TPU v7x, 32 devices: a whole 2x2x4 slice. The times are simulated.
32 devices in a mesh: band: 2 (over x), ens: 16 (over z, y, core).
Axes of the slice: x: 2, y: 2, z: 4, core: 2. Of those that a mesh axis runs over, the one named last changes fastest.
Arguments:
- fine_state: bfloat16 [64, 8, 16, 512], P('ens', None, 'band'), may hold values from -5 to 5
- coarse_state: bfloat16 [64, 8, 4, 128], P('ens', None, 'band'), may hold values from -5 to 5
- noise: bfloat16 [2, 64, 8, 16, 512], P(None, 'ens', None, 'band'), may hold values from -5 to 5
- kernel_fine: bfloat16 [8, 72], replicated, may hold values from -0.75 to 0.75
- kernel_coarse: bfloat16 [8, 72], replicated, may hold values from -0.75 to 0.75
- obs_fine: bfloat16 [8, 16, 512], P(None, 'band'), may hold values from -5 to 6
- obs_coarse: bfloat16 [8, 4, 128], P(None, 'band'), may hold values from -5 to 6
- precision_fine: float32 [16], P('band'), may hold values from 0.3 to 14, as said below
- precision_coarse: float32 [4], P('band'), may hold values from 0.3 to 14, as said below
- offspring: int32 [64], replicated, may hold values from 0 to 8, as said below
- dest_slot: int32 [64], replicated, may hold values from 0 to 63, each once
Outputs:
- fine_next: bfloat16 [64, 8, 16, 512], P('ens', None, 'band')
- coarse_next: bfloat16 [64, 8, 4, 128], P('ens', None, 'band')
- logw_fine: float32 [64], P('ens')
- logw_coarse: float32 [64], P('ens')
Inputs may be any that keep to these rules, and one draw needn't show every extreme that they name: non-negative offspring counts that sum to 64; the counts of each aligned block of 8 pairs sum to 8. `dest_slot`: each slot appears once. `precision_fine`: positive. `precision_coarse`: positive.
All inputs are finite; a program needn't handle non-finite values.
Results may differ from a plain program's by a relative error of at most 0.0049.
Values may be sent and summed in bfloat16 or wider, within the bound.
A program may use at most 64 MiB of HBM per device.

v0:
```python
import jax
import jax.numpy as jnp
from jax import lax
from jax.sharding import PartitionSpec as P


def padded_2(block, sides, width):
    for axis, dim in sides:
        count = lax.axis_size(axis)
        forward = [(i, i + 1) for i in range(count - 1)]
        backward = [(target, source) for source, target in forward]
        low = lax.ppermute(
            lax.slice_in_dim(block, block.shape[dim] - width, None, axis=dim), axis, forward
        )
        high = lax.ppermute(lax.slice_in_dim(block, 0, width, axis=dim), axis, backward)
        block = jnp.concatenate([low, block, high], axis=dim)
    return block


def conv_taps(padded, rows):
    stack = []
    for shift_row in range(3):
        band_rows = padded[:, :, shift_row : shift_row + rows, :]
        for shift_col in (-1, 0, 1):
            stack.append(jnp.roll(band_rows, -shift_col, axis=3))
    joined = jnp.stack(stack, axis=2)
    return joined.reshape(joined.shape[0], joined.shape[1] * 9, rows, joined.shape[4])


def advance(state, padded, forcing, kernel):
    taps = conv_taps(padded, state.shape[2])
    mixed = jnp.einsum("ok,pkrl->porl", kernel, taps, preferred_element_type=jnp.float32)
    return (state.astype(jnp.float32) + 0.5 * jnp.tanh(mixed + forcing)).astype(jnp.bfloat16)


def step_fine(state, forcing, kernel):
    padded = padded_2(state, (("band", 2),), 1)
    return advance(state, padded, forcing, kernel)


def step_coarse(state, forcing, kernel):
    padded = padded_2(state, (("band", 2),), 1)
    return advance(state, padded, forcing, kernel)


def restrict(field):
    shape = field.shape
    blocks = field.reshape(shape[0], shape[1], shape[2] // 4, 4, shape[3] // 4, 4)
    return 4.0 * jnp.mean(blocks, axis=(3, 5))


def misfit(state, observed, precision, scale):
    diff = state.astype(jnp.float32) - observed.astype(jnp.float32)[None]
    return -0.5 * scale * jnp.sum(precision[None, None, :, None] * diff * diff, axis=(1, 2, 3))


def shards(
    fine_state,
    coarse_state,
    noise,
    kernel_fine,
    kernel_coarse,
    obs_fine,
    obs_coarse,
    precision_fine,
    precision_coarse,
    offspring,
    dest_slot,
):
    bands = lax.axis_size("band")
    members = lax.axis_size("ens")
    per_dev = fine_state.shape[0]
    for step in range(noise.shape[0]):
        forcing = noise[step].astype(jnp.float32)
        fine_state = step_fine(fine_state, forcing, kernel_fine)
        coarse_state = step_coarse(coarse_state, restrict(forcing), kernel_coarse)
    channels = fine_state.shape[1]
    fine_cells = channels * fine_state.shape[2] * bands * fine_state.shape[3]
    coarse_cells = channels * coarse_state.shape[2] * bands * coarse_state.shape[3]
    scale_fine = 1.0 / jnp.sqrt(jnp.float32(fine_cells))
    scale_coarse = 1.0 / jnp.sqrt(jnp.float32(coarse_cells))
    fine_part = misfit(fine_state, obs_fine, precision_fine, scale_fine)
    coarse_part = misfit(coarse_state, obs_coarse, precision_coarse, scale_coarse)
    like_fine, like_coarse = lax.psum((fine_part, coarse_part), "band")
    peak_fine, peak_coarse = lax.pmax((jnp.max(like_fine), jnp.max(like_coarse)), "ens")
    total_fine, total_coarse = lax.psum(
        (jnp.sum(jnp.exp(like_fine - peak_fine)), jnp.sum(jnp.exp(like_coarse - peak_coarse))),
        "ens",
    )
    logw_fine = like_fine - (peak_fine + jnp.log(total_fine))
    logw_coarse = like_coarse - (peak_coarse + jnp.log(total_coarse))
    total_slots = offspring.shape[0]
    order = jnp.arange(total_slots, dtype=jnp.int32)
    ends = jnp.cumsum(offspring)
    parent = jnp.sum((ends[None, :] <= order[:, None]).astype(jnp.int32), axis=1)
    slot_parent = jnp.sum(
        jnp.where(dest_slot[None, :] == order[:, None], parent[None, :], 0), axis=1
    )
    selector = (slot_parent[:, None] == order[None, :]).astype(jnp.bfloat16)
    fine_flat = fine_state.reshape(per_dev, members, -1)
    chosen = jnp.einsum(
        "so,oxc->sxc",
        selector,
        lax.all_to_all(fine_flat, "ens", split_axis=1, concat_axis=0, tiled=True),
        preferred_element_type=jnp.float32,
    ).astype(jnp.bfloat16)
    moved = lax.all_to_all(chosen, "ens", split_axis=0, concat_axis=1, tiled=True)
    fine_next = moved.reshape(fine_state.shape)
    everyone = lax.all_gather(coarse_state, "ens", axis=0, tiled=True)
    mine = lax.dynamic_slice_in_dim(selector, lax.axis_index("ens") * per_dev, per_dev, 0)
    coarse_next = jnp.einsum(
        "so,ocrl->scrl", mine, everyone, preferred_element_type=jnp.float32
    ).astype(jnp.bfloat16)
    return (fine_next, coarse_next, logw_fine, logw_coarse)


def solution(mesh):
    return jax.shard_map(
        shards,
        mesh=mesh,
        in_specs=(
            P("ens", None, "band", None),
            P("ens", None, "band", None),
            P(None, "ens", None, "band", None),
            P(),
            P(),
            P(None, "band", None),
            P(None, "band", None),
            P("band"),
            P("band"),
            P(),
            P(),
        ),
        out_specs=(P("ens", None, "band", None), P("ens", None, "band", None), P("ens"), P("ens")),
        check_vma=False,
    )
```

profile of v0, /device:TPU:0, one launch (start us, length us, event | category | flops | bytes accessed | tf_op | source)
XLA Modules:
  0.0 179.7 jit_solution(7127977191837988565)
XLA Ops:
  0.6 1.2 fusion.129
  1.8 4.8 %collective-permute-start = (bf16[4,8,1,512]{3,2,1,0:T(2,128)(2,1)S(1)}, bf16[4,8,1,512]{3,2,1,0:T(2,128)(2,1)S(1)}, u32[]{:S(2)}, u32[]{:S(2)}) collective-permute-start(bf16[4,8,1,512]{3,2,1,0:T(2,128)(2,1)S(1)} %get-tuple-element.57), channel_id=1, source_target_pairs={{0,16},{1,17},{2,18},{3,19},{4,20},{5,21},{6,22},{7,23},{8,24},{9,... | collective-permute-start | bytes 98312 | tf_op jit(solution)/shard_map/ppermute | solution.py:12
  6.7 1.3 collective-permute-start.1
  8.0 0.8 fusion.133
  8.8 1.3 collective-permute-start.5
  10.1 4.5 %collective-permute-start.4 = (bf16[4,8,1,128]{3,2,1,0:T(2,128)(2,1)S(1)}, bf16[4,8,1,128]{3,2,1,0:T(2,128)(2,1)S(1)}, u32[]{:S(2)}, u32[]{:S(2)}) collective-permute-start(bf16[4,8,1,128]{3,2,1,0:T(2,128)(2,1)S(1)} %get-tuple-element.91), channel_id=1, source_target_pairs={{0,16},{1,17},{2,18},{3,19},{4,20},{5,21},{6,22},{7,23},{8,24},{9,... | collective-permute-start | bytes 24584 | tf_op jit(solution)/shard_map/ppermute | solution.py:12
  14.7 1.0 fusion.131
  15.6 1.1 fusion.125
  16.7 0.7 copy.135
  17.8 0.8 select_reduce_fusion
  18.8 4.6 %copy.153 = f32[1,4,8,8,512]{2,4,3,1,0:T(8,128)} copy(f32[1,4,8,8,512]{4,2,3,1,0:T(8,128)S(1)} %get-tuple-element.97) | data formatting | bytes 1048576 | tf_op jit(solution)/shard_map/convert_element_type | solution.py:74
  23.4 6.3 %reduce_sum.74 = f32[4,8,2,128]{1,3,2,0:T(8,128)S(1)} reduce(f32[4,8,2,4,128,4]{1,5,4,3,2,0:T(4,128)} %bitcast.234, f32[]{:T(128)} %constant.8.clone.1), dimensions={3,5}, to_apply=%region_3.4 | reduce | flops 122880 | bytes 557060 | tf_op jit(solution)/shard_map/reduce_sum | solution.py:49
  29.9 0.2 fusion.104
  31.4 1.3 collective-permute-start.7
  32.7 4.7 %collective-permute-start.6 = (bf16[4,8,1,128]{3,1,2,0:T(8,128)(2,1)S(1)}, bf16[4,8,1,128]{3,1,2,0:T(8,128)(2,1)S(1)}, u32[]{:S(2)}, u32[]{:S(2)}) collective-permute-start(bf16[4,8,1,128]{3,1,2,0:T(8,128)(2,1)S(1)} %get-tuple-element.81), channel_id=1, source_target_pairs={{0,16},{1,17},{2,18},{3,19},{4,20},{5,21},{6,22},{7,23},{8,24},{9,... | collective-permute-start | bytes 24584 | tf_op jit(solution)/shard_map/ppermute | solution.py:12
  37.5 4.6 %copy.157 = f32[1,4,8,8,512]{2,4,3,1,0:T(8,128)} copy(f32[1,4,8,8,512]{4,2,3,1,0:T(8,128)S(1)} %get-tuple-element.96) | data formatting | bytes 1048576 | tf_op jit(solution)/shard_map/convert_element_type | solution.py:74
  42.1 6.2 %reduce_sum.75 = f32[4,8,2,128]{1,3,2,0:T(8,128)S(1)} reduce(f32[4,8,2,4,128,4]{1,5,4,3,2,0:T(4,128)} %bitcast.233, f32[]{:T(128)} %constant.8.clone.1), dimensions={3,5}, to_apply=%region_4.5 | reduce | flops 122880 | bytes 557060 | tf_op jit(solution)/shard_map/reduce_sum | solution.py:49
  49.4 0.2 fusion.93
  49.8 0.2 fusion.126
  50.1 0.5 fusion.130
  51.6 0.8 fusion.35
  52.5 1.3 collective-permute-start.3
  53.8 4.5 %collective-permute-start.2 = (bf16[4,8,1,512]{3,1,2,0:T(8,128)(2,1)S(1)}, bf16[4,8,1,512]{3,1,2,0:T(8,128)(2,1)S(1)}, u32[]{:S(2)}, u32[]{:S(2)}) collective-permute-start(bf16[4,8,1,512]{3,1,2,0:T(8,128)(2,1)S(1)} %get-tuple-element.55), channel_id=1, source_target_pairs={{0,16},{1,17},{2,18},{3,19},{4,20},{5,21},{6,22},{7,23},{8,24},{9,... | collective-permute-start | bytes 98312 | tf_op jit(solution)/shard_map/ppermute | solution.py:12
  58.4 1.6 collective-permute-done.2
  59.9 0.3 fusion.52
  61.2 0.8 copy.143
  62.0 1.0 fusion.51
  63.2 0.9 copy.147
  64.2 5.9 %all-to-all-start = ((bf16[4,16,2048]{2,0,1:T(4,128)(2,1)}), bf16[4,16,2048]{2,0,1:T(4,128)(2,1)S(1)}, u32[]{:S(2)}, u32[]{:S(2)}) async-start(bf16[4,16,2048]{2,0,1:T(4,128)(2,1)} %copy.147), calls=%async_computation | async-start | bytes 524288 | tf_op jit(solution)/shard_map/all_to_all | solution.py:104
  70.1 22.5 %all_gather.3 = bf16[64,8,2,128]{3,1,2,0:T(8,128)(2,1)S(1)} all-gather(bf16[4,8,2,128]{3,1,2,0:T(8,128)(2,1)S(1)} %get-tuple-element.95), channel_id=1, replica_groups=mesh['band'=2,'ens'=16] {'ens'}, dimensions={0}, use_global_device_ids=true | all-gather | bytes 278528 | tf_op jit(solution)/shard_map/all_gather | solution.py:109
  92.6 5.2 %all-reduce.2 = (f32[4]{0:T(128)S(1)}, f32[4]{0:T(128)S(1)}) all-reduce(f32[4]{0:T(128)S(1)} %broadcast_multiply_fusion.1, f32[4]{0:T(128)S(1)} %broadcast_multiply_fusion), channel_id=1, replica_groups=mesh['band'=2,'ens'=16] {'band'}, use_global_device_ids=true, to_apply=%region_6.7 | all-reduce | flops 8 | bytes 64 | tf_op jit(solution)/shard_map/psum | solution.py:84
  97.8 0.6 reduce_max.18
  98.4 0.6 reduce_max.19
  99.2 30.2 %all-reduce.1 = (f32[]{:T(128)}, f32[]{:T(128)}) all-reduce(f32[]{:T(128)} %reduce_max.18, f32[]{:T(128)} %reduce_max.19), channel_id=1, replica_groups=mesh['band'=2,'ens'=16] {'ens'}, use_global_device_ids=true, to_apply=%region_8.9 | all-reduce | flops 2 | bytes 16 | tf_op jit(solution)/shard_map/pmax | solution.py:85
  129.4 1.3 exponential_reduce_fusion.1
  130.8 0.3 fusion.4
  131.1 0.5 broadcast.37
  131.6 0.8 reduce.2
  132.3 0.9 reshape.94
  133.3 3.5 %all-to-all-start.1 = ((bf16[16,2,4096]{2,1,0:T(2,128)(2,1)}), bf16[16,2,4096]{2,1,0:T(2,128)(2,1)S(1)}, u32[]{:S(2)}, u32[]{:S(2)}) async-start(bf16[16,2,4096]{2,1,0:T(2,128)(2,1)} %reshape.94), calls=%async_computation.1 | async-start | bytes 524288 | tf_op jit(solution)/shard_map/all_to_all | solution.py:107
  136.8 1.3 exponential_reduce_fusion
  138.1 0.6 copy.162
  138.7 34.4 %all-reduce = (f32[]{:T(128)}, f32[]{:T(128)}) all-reduce(f32[]{:T(128)} %exponential_reduce_fusion.1, f32[]{:T(128)} %exponential_reduce_fusion), channel_id=1, replica_groups=mesh['band'=2,'ens'=16] {'ens'}, use_global_device_ids=true, to_apply=%region_10.11 | all-reduce | flops 2 | bytes 16 | tf_op jit(solution)/shard_map/psum | solution.py:86
  175.7 0.5 broadcast_subtract_fusion.1
  176.3 0.5 broadcast_subtract_fusion
  176.8 0.3 reshape.95
  177.0 1.5 reduce.1
  178.9 0.9 reshape.82
  (90 shorter events, 5.9 us)
Async XLA Ops:
  0.6 51.0 %copy-start = (bf16[8,72]{1,0:T(8,128)(2,1)S(1)}, bf16[8,72]{1,0:T(8,128)(2,1)}, u32[]{:S(2)}) copy-start(bf16[8,72]{1,0:T(8,128)(2,1)} %param.14) | copy-start | bytes 3460
  1.8 48.3 %collective-permute-start = (bf16[4,8,1,512]{3,2,1,0:T(2,128)(2,1)S(1)}, bf16[4,8,1,512]{3,2,1,0:T(2,128)(2,1)S(1)}, u32[]{:S(2)}, u32[]{:S(2)}) collective-permute-start(bf16[4,8,1,512]{3,2,1,0:T(2,128)(2,1)S(1)} %get-tuple-element.57), channel_id=1, source_target_pairs={{0,16},{1,17},{2,18},{3,19},{4,20},{5,21},{6,22},{7,23},{8,24},{9,... | collective-permute-start | bytes 98312 | tf_op jit(solution)/shard_map/ppermute | solution.py:12
  6.7 43.0 %collective-permute-start.1 = (bf16[4,8,1,512]{3,2,1,0:T(2,128)(2,1)S(1)}, bf16[4,8,1,512]{3,2,1,0:T(2,128)(2,1)S(1)}, u32[]{:S(2)}, u32[]{:S(2)}) collective-permute-start(bf16[4,8,1,512]{3,2,1,0:T(2,128)(2,1)S(1)} %get-tuple-element.56), channel_id=1, source_target_pairs={{16,0},{17,1},{18,2},{19,3},{20,4},{21,5},{22,6},{23,7},{24,8},{25... | collective-permute-start | bytes 98312 | tf_op jit(solution)/shard_map/ppermute | solution.py:15
  8.8 21.1 %collective-permute-start.5 = (bf16[4,8,1,128]{3,2,1,0:T(2,128)(2,1)S(1)}, bf16[4,8,1,128]{3,2,1,0:T(2,128)(2,1)S(1)}, u32[]{:S(2)}, u32[]{:S(2)}) collective-permute-start(bf16[4,8,1,128]{3,2,1,0:T(2,128)(2,1)S(1)} %get-tuple-element.90), channel_id=1, source_target_pairs={{16,0},{17,1},{18,2},{19,3},{20,4},{21,5},{22,6},{23,7},{24,8},{25... | collective-permute-start | bytes 24584 | tf_op jit(solution)/shard_map/ppermute | solution.py:15
  10.1 19.8 %collective-permute-start.4 = (bf16[4,8,1,128]{3,2,1,0:T(2,128)(2,1)S(1)}, bf16[4,8,1,128]{3,2,1,0:T(2,128)(2,1)S(1)}, u32[]{:S(2)}, u32[]{:S(2)}) collective-permute-start(bf16[4,8,1,128]{3,2,1,0:T(2,128)(2,1)S(1)} %get-tuple-element.91), channel_id=1, source_target_pairs={{0,16},{1,17},{2,18},{3,19},{4,20},{5,21},{6,22},{7,23},{8,24},{9,... | collective-permute-start | bytes 24584 | tf_op jit(solution)/shard_map/ppermute | solution.py:12
  23.4 6.5 %copy-start.2 = (bf16[4,8,2,128]{3,2,1,0:T(2,128)(2,1)S(1)}, bf16[4,8,2,128]{3,2,1,0:T(2,128)(2,1)}, u32[]{:S(2)}) copy-start(bf16[4,8,2,128]{3,2,1,0:T(2,128)(2,1)} %param.12) | copy-start | bytes 49156
  23.4 7.8 %copy-start.5 = (bf16[8,72]{1,0:T(8,128)(2,1)S(1)}, bf16[8,72]{1,0:T(8,128)(2,1)}, u32[]{:S(2)}) copy-start(bf16[8,72]{1,0:T(8,128)(2,1)} %param.15) | copy-start | bytes 3460
  23.4 14.0 %copy-start.1 = (bf16[4,8,8,512]{3,2,1,0:T(8,128)(2,1)S(1)}, bf16[4,8,8,512]{3,2,1,0:T(8,128)(2,1)}, u32[]{:S(2)}) copy-start(bf16[4,8,8,512]{3,2,1,0:T(8,128)(2,1)} %param.11) | copy-start | bytes 786436
  29.7 7.8 %copy-start.3 = (bf16[8,8,512]{2,1,0:T(8,128)(2,1)S(1)}, bf16[8,8,512]{2,1,0:T(8,128)(2,1)}, u32[]{:S(2)}) copy-start(bf16[8,8,512]{2,1,0:T(8,128)(2,1)} %param.16) | copy-start | bytes 196612
  29.7 7.8 %copy-start.4 = (bf16[8,2,128]{2,1,0:T(2,128)(2,1)S(1)}, bf16[8,2,128]{2,1,0:T(2,128)(2,1)}, u32[]{:S(2)}) copy-start(bf16[8,2,128]{2,1,0:T(2,128)(2,1)} %param.17) | copy-start | bytes 12292
  31.4 17.1 %collective-permute-start.7 = (bf16[4,8,1,128]{3,1,2,0:T(8,128)(2,1)S(1)}, bf16[4,8,1,128]{3,1,2,0:T(8,128)(2,1)S(1)}, u32[]{:S(2)}, u32[]{:S(2)}) collective-permute-start(bf16[4,8,1,128]{3,1,2,0:T(8,128)(2,1)S(1)} %get-tuple-element.80), channel_id=1, source_target_pairs={{16,0},{17,1},{18,2},{19,3},{20,4},{21,5},{22,6},{23,7},{24,8},{25... | collective-permute-start | bytes 24584 | tf_op jit(solution)/shard_map/ppermute | solution.py:15
  32.7 15.8 %collective-permute-start.6 = (bf16[4,8,1,128]{3,1,2,0:T(8,128)(2,1)S(1)}, bf16[4,8,1,128]{3,1,2,0:T(8,128)(2,1)S(1)}, u32[]{:S(2)}, u32[]{:S(2)}) collective-permute-start(bf16[4,8,1,128]{3,1,2,0:T(8,128)(2,1)S(1)} %get-tuple-element.81), channel_id=1, source_target_pairs={{0,16},{1,17},{2,18},{3,19},{4,20},{5,21},{6,22},{7,23},{8,24},{9,... | collective-permute-start | bytes 24584 | tf_op jit(solution)/shard_map/ppermute | solution.py:12
  42.1 7.3 %copy-start.6 = (f32[2]{0:T(128)S(1)}, f32[2]{0:T(128)}, u32[]{:S(2)}) copy-start(f32[2]{0:T(128)} %param.19) | copy-start | bytes 28
  52.5 5.9 %collective-permute-start.3 = (bf16[4,8,1,512]{3,1,2,0:T(8,128)(2,1)S(1)}, bf16[4,8,1,512]{3,1,2,0:T(8,128)(2,1)S(1)}, u32[]{:S(2)}, u32[]{:S(2)}) collective-permute-start(bf16[4,8,1,512]{3,1,2,0:T(8,128)(2,1)S(1)} %get-tuple-element.54), channel_id=1, source_target_pairs={{16,0},{17,1},{18,2},{19,3},{20,4},{21,5},{22,6},{23,7},{24,8},{25... | collective-permute-start | bytes 98312 | tf_op jit(solution)/shard_map/ppermute | solution.py:15
  53.8 6.1 %collective-permute-start.2 = (bf16[4,8,1,512]{3,1,2,0:T(8,128)(2,1)S(1)}, bf16[4,8,1,512]{3,1,2,0:T(8,128)(2,1)S(1)}, u32[]{:S(2)}, u32[]{:S(2)}) collective-permute-start(bf16[4,8,1,512]{3,1,2,0:T(8,128)(2,1)S(1)} %get-tuple-element.55), channel_id=1, source_target_pairs={{0,16},{1,17},{2,18},{3,19},{4,20},{5,21},{6,22},{7,23},{8,24},{9,... | collective-permute-start | bytes 98312 | tf_op jit(solution)/shard_map/ppermute | solution.py:12
  61.2 0.8 copy-start.7
  64.2 66.6 %all-to-all-start = ((bf16[4,16,2048]{2,0,1:T(4,128)(2,1)}), bf16[4,16,2048]{2,0,1:T(4,128)(2,1)S(1)}, u32[]{:S(2)}, u32[]{:S(2)}) async-start(bf16[4,16,2048]{2,0,1:T(4,128)(2,1)} %copy.147), calls=%async_computation | async-start | bytes 524288 | tf_op jit(solution)/shard_map/all_to_all | solution.py:104
  133.3 43.5 %all-to-all-start.1 = ((bf16[16,2,4096]{2,1,0:T(2,128)(2,1)}), bf16[16,2,4096]{2,1,0:T(2,128)(2,1)S(1)}, u32[]{:S(2)}, u32[]{:S(2)}) async-start(bf16[16,2,4096]{2,1,0:T(2,128)(2,1)} %reshape.94), calls=%async_computation.1 | async-start | bytes 524288 | tf_op jit(solution)/shard_map/all_to_all | solution.py:107
where the time goes:
time: 181 us; the launch traced here: 180 us
  blocking collectives  92.4 us (51%)
  starting transfers between devices  33.3 us (18%)
  other arithmetic  25.3 us (14%)
  local copies, waits for them, and re-layouts  20.7 us (11%)
  between operations  3.85 us (2%)
  matrix products  2.62 us (1%)
    psum x1, blocking collectives, shards(): lax.psum((jnp.sum(jnp.exp(like_fine - peak_fine)), jnp.sum(jnp.exp(like_c...  34.4 us
    pmax x1, blocking collectives, shards(): lax.pmax((jnp.max(like_fine), jnp.max(like_coarse)), 'ens')  30.2 us
    all_gather x1, blocking collectives, shards(): everyone = lax.all_gather(coarse_state, 'ens', axis=0, tiled=True)  22.5 us
    ppermute x4, starting transfers between devices, padded_2(): lax.ppermute(lax.slice_in_dim(block, block.shape[dim] - width, None, axis...  18.7 us
    reduce_sum x2, other arithmetic, restrict(): return 4.0 * jnp.mean(blocks, axis=(3, 5))  12.5 us
    convert_element_type x2, local copies, waits for them, and re-layouts, shards(): forcing = noise[step].astype(jnp.float32)  9.18 us
    all_to_all x1, starting transfers between devices, shards(): lax.all_to_all(fine_flat, 'ens', split_axis=1, concat_axis=0, tiled=True)  5.94 us
    psum x1, blocking collectives, shards(): like_fine, like_coarse = lax.psum((fine_part, coarse_part), 'band')  5.19 us
  transfers between devices with their start and end apart: 10, of which 1 were waited for; matrix products, arithmetic and copies ran while one was open for 20% of the time, Pallas kernels for 0%

commit v1 on v0

v1 whole, which is shorter than its diff:
```python
import functools
import math

import jax
import jax.numpy as jnp
from jax import lax
from jax.experimental import pallas as pl
from jax.experimental.pallas import tpu as pltpu
from jax.sharding import PartitionSpec as P

F32 = jnp.float32
BF16 = jnp.bfloat16
I32 = jnp.int32
TILE_R = 16
TILE_L = 128


def iota(shape, dim):
    return lax.broadcasted_iota(I32, shape, dim)


def onehot(cond):
    return jnp.where(cond, 1.0, 0.0).astype(BF16)


def mm(a, b):
    return jnp.dot(a, b, preferred_element_type=F32)


def layout(idx, ch, rows, halo):
    base = ch * rows
    own_c, own_r = idx >> int(math.log2(rows)), idx & (rows - 1)
    if halo == 0:
        return own_c, own_r
    up = idx - base
    down = up - halo * ch
    above = -1 - jnp.where(up >= ch, 1, 0)
    below = rows + jnp.where(down >= ch, 1, 0)
    side_c = up & (ch - 1)
    side_r = jnp.where(down < 0, above, below)
    return jnp.where(idx < base, own_c, side_c), jnp.where(idx < base, own_r, side_r)


def conv_matrix(kern, ch, rows, halo_out, halo_in):
    n_out = ch * (rows + 2 * halo_out)
    n_in = ch * (rows + 2 * halo_in)
    o, r_out = layout(iota((n_out, 1), 0), ch, rows, halo_out)
    col = iota((1, 3 * n_in), 1)
    shift = jnp.where(col >= n_in, 1, 0) + jnp.where(col >= 2 * n_in, 1, 0)
    i, r_in = layout(col - n_in * shift, ch, rows, halo_in)
    spread = mm(onehot(o == iota((n_out, ch), 1)), kern).astype(BF16)
    taps = iota((9 * ch, 3 * n_in), 0)
    total = None
    for a in range(3):
        pick = mm(spread, onehot(taps == 9 * i + 3 * a + shift))
        term = jnp.where(r_in - r_out + 1 == a, pick, 0.0)
        total = term if total is None else total + term
    return total.astype(BF16)


def shifted(x, width):
    parts = [x[:, j : j + width] for j in range(0, x.shape[1], width)]
    left = [pltpu.roll(v, 1, 1) for v in parts]
    right = [pltpu.roll(v, width - 1, 1) for v in parts]
    join = lambda vs: vs[0] if len(vs) == 1 else jnp.concatenate(vs, axis=1)
    return jnp.concatenate([join(left), x, join(right)], axis=0).astype(BF16)


def kernel(
    bands, members,
    fine, coarse, noise, kf, kc, obs_f, obs_c, prec_f, prec_c, offs, dest,
    out_f, out_c, out_lf, out_lc,
    halo_tx, halo_rx, edge_tx, edge_rx, fin, recv1, chosen, cstage, recvc, cchosen, recvc2,
    likeb, likee, par_v, par_s,
    h_send, h_recv, e_send, e_recv, s1, r1, s2, r2, cs1, cr1, cs2, cr2, bs, br, ls, lr, loc,
):
    band = lax.axis_index("band")
    me = lax.axis_index("ens")
    n_p, ch, hf, lon = fine.shape[0], kf.shape[0], prec_f.shape[1], fine.shape[2]
    hc, lonc = prec_c.shape[1], coarse.shape[1]
    rf, rc = ch * hf, ch * hc
    lane_blocks = lon // TILE_L
    shares = (rf // TILE_R) * lane_blocks
    holders = n_p * rc // TILE_R
    piece = rc // holders
    total = offs.shape[1]
    group = (me // shares) * shares
    rank = me - group

    def holder(c):
        return c * (shares // holders) + (c % 2) * (shares // holders // 2)

    def tile(ref, share):
        row = pl.multiple_of((share // lane_blocks) * TILE_R, TILE_R)
        lane = pl.multiple_of((share % lane_blocks) * TILE_L, TILE_L)
        return ref.at[:, pl.ds(row, TILE_R), pl.ds(lane, TILE_L)]

    def copy_to(src, dst, send, recv, device):
        return pltpu.make_async_remote_copy(
            src_ref=src, dst_ref=dst, send_sem=send, recv_sem=recv,
            device_id=device, device_id_type=pl.DeviceIdType.MESH,
        )

    barrier = pltpu.get_barrier_semaphore()
    for k in range(1, members):
        pl.semaphore_signal(barrier, inc=1, device_id={"ens": lax.rem(me + k, members)},
                            device_id_type=pl.DeviceIdType.MESH)
    for k in range(1, bands):
        pl.semaphore_signal(barrier, inc=1, device_id={"band": lax.rem(band + k, bands)},
                            device_id_type=pl.DeviceIdType.MESH)

    def edge_rows(n_side, rows):
        q = iota((2 * n_side, ch * rows), 0)
        lower = q >= n_side
        t = jnp.where(lower, q - n_side, q)
        depth = jnp.where(t >= ch, 1, 0)
        row = jnp.where(lower, rows - 1 - depth, depth)
        return onehot(iota((2 * n_side, ch * rows), 1) == (t & (ch - 1)) * rows + row)

    sel_state, sel_noise, sel_coarse = edge_rows(2 * ch, hf), edge_rows(ch, hf), edge_rows(2 * ch, hc)
    n_base = n_p * 2 * ch
    c_base = n_base + n_p * ch
    picked_noise = []
    for p in range(n_p):
        rows = mm(sel_state, fine[p]).astype(BF16)
        halo_tx[0, pl.ds(p * 2 * ch, 2 * ch), :] = rows[: 2 * ch]
        halo_tx[1, pl.ds(p * 2 * ch, 2 * ch), :] = rows[2 * ch :]
        picked_noise.append(mm(sel_noise, noise[0, p]))
    for side in range(2):
        halo_tx[side, pl.ds(n_base, n_p * ch), :] = jnp.concatenate(
            [v[side * ch : (side + 1) * ch] for v in picked_noise], axis=0
        ).astype(BF16)
    c0 = jnp.concatenate([coarse[pl.ds(p * rc, rc), :] for p in range(n_p)], axis=1)
    rows = mm(sel_coarse, c0).astype(BF16)
    halo_tx[0, pl.ds(c_base, 2 * ch), :] = rows[: 2 * ch]
    halo_tx[1, pl.ds(c_base, 2 * ch), :] = rows[2 * ch :]

    pl.semaphore_wait(barrier, members + bands - 2)

    up, down = lax.max(band - 1, 0), lax.min(band + 1, bands - 1)
    has_up, has_down = band > 0, band < bands - 1

    def pair(tx, rx, send, recv, side):
        return copy_to(tx.at[side], rx.at[1 - side], send.at[side], recv.at[1 - side],
                       {"band": up if side == 0 else down})

    halo = [pair(halo_tx, halo_rx, h_send, h_recv, side) for side in range(2)]
    edge = [pair(edge_tx, edge_rx, e_send, e_recv, side) for side in range(2)]

    @pl.when(has_up)
    def _():
        halo[0].start()

    @pl.when(has_down)
    def _():
        halo[1].start()

    r4 = hf // hc
    q = iota((rc + 2 * ch, rf), 0)
    cell_c = jnp.where(q < rc, q >> int(math.log2(hc)), (q - rc) & (ch - 1))
    cell_r = jnp.where(q < rc, q & (hc - 1), jnp.where(q < rc + ch, 0, hc - 1))
    src = iota((rc + 2 * ch, rf), 1)
    gather_rows = onehot((src >> int(math.log2(r4))) == cell_c * hc + cell_r)
    l4 = lon // lonc
    fold = onehot((iota((lon, lonc), 0) >> int(math.log2(l4))) == iota((lon, lonc), 1))
    sums = jnp.concatenate(
        [mm(gather_rows, noise[s, p]) for s in range(2) for p in range(n_p)], axis=0
    )
    hi = sums.astype(BF16)
    rest = sums - hi.astype(F32)
    mid = rest.astype(BF16)
    low = (rest - mid.astype(F32)).astype(BF16)
    scale_r = 4.0 / (r4 * l4)
    folded = (mm(hi, fold) + (mm(mid, fold) + mm(low, fold))) * scale_r
    block = rc + 2 * ch

    def forcing_rows(step, lo, n):
        return jnp.concatenate(
            [folded[(step * n_p + p) * block + lo : (step * n_p + p) * block + lo + n] for p in range(n_p)],
            axis=1,
        )

    edge_tx[0] = forcing_rows(0, rc, ch)
    edge_tx[1] = forcing_rows(0, rc + ch, ch)

    @pl.when(has_up)
    def _():
        edge[0].start()

    @pl.when(has_down)
    def _():
        edge[1].start()

    lane_w = par_v.shape[1]
    lanes = iota((total, total), 1)
    subs = iota((total, total), 0)
    ends = jnp.sum(jnp.where(lanes <= subs, offs[...], 0), axis=1, keepdims=True)
    parent = jnp.sum(jnp.where(ends <= lanes, 1, 0), axis=0, keepdims=True)
    slot_col = jnp.sum(jnp.where(dest[...] == subs, parent, 0), axis=1, keepdims=True)
    par_v[...] = jnp.sum(
        jnp.where(iota((total, lane_w), 0) == iota((total, lane_w), 1), jnp.minimum(slot_col, total - 1), 0),
        axis=0, keepdims=True,
    )
    to_smem = pltpu.make_async_copy(par_v, par_s, loc.at[0])
    to_smem.start()

    w1 = conv_matrix(kf[...], ch, hf, 1, 2)
    w2 = conv_matrix(kf[...], ch, hf, 0, 1)
    w1c = conv_matrix(kc[...], ch, hc, 1, 2)
    w2c = conv_matrix(kc[...], ch, hc, 0, 1)
    pf = jnp.sum(jnp.where(iota((rf, hf), 1) == (iota((rf, hf), 0) & (hf - 1)), prec_f[...], 0.0), axis=1, keepdims=True)
    pc = jnp.sum(jnp.where(iota((rc, hc), 1) == (iota((rc, hc), 0) & (hc - 1)), prec_c[...], 0.0), axis=1, keepdims=True)
    to_smem.wait()

    @pl.when(jnp.logical_not(has_up))
    def _():
        halo_rx[0] = jnp.zeros(halo_rx.shape[1:], BF16)
        edge_rx[0] = jnp.zeros(edge_rx.shape[1:], F32)

    @pl.when(jnp.logical_not(has_down))
    def _():
        halo_rx[1] = jnp.zeros(halo_rx.shape[1:], BF16)
        edge_rx[1] = jnp.zeros(edge_rx.shape[1:], F32)

    def pair_wait(pairs, which):
        for side in range(2):
            @pl.when((has_up, has_down)[side])
            def _():
                if which == "recv":
                    pairs[1 - side].wait_recv()
                else:
                    pairs[side].wait_send()

    pair_wait(halo, "recv")

    q = iota((ch * (hf + 2), 1), 0)
    keep_f = jnp.logical_and(
        jnp.logical_or(has_up, jnp.logical_or(q < rf, q >= rf + ch)), jnp.logical_or(has_down, q < rf + ch)
    )
    q = iota((ch * (hc + 2), 1), 0)
    keep_c = jnp.logical_and(
        jnp.logical_or(has_up, jnp.logical_or(q < rc, q >= rc + ch)), jnp.logical_or(has_down, q < rc + ch)
    )

    def two_steps(own, above, below, force0, force1, wa, wb, keep, width):
        x = jnp.concatenate([own, above, below], axis=0)
        mixed = mm(wa, shifted(x, width))
        base = jnp.concatenate([own, above[:ch], below[:ch]], axis=0)
        y = (base + 0.5 * jnp.tanh(mixed + force0)).astype(BF16).astype(F32)
        y = jnp.where(keep, y, 0.0)
        mixed = mm(wb, shifted(y, width))
        return (y[: own.shape[0]] + 0.5 * jnp.tanh(mixed + force1)).astype(BF16)

    lane = iota((1, TILE_L), 1)
    like = jnp.zeros((1, TILE_L), F32)
    scale_f = -0.5 / math.sqrt(ch * hf * bands * lon)
    scale_c = -0.5 / math.sqrt(ch * hc * bands * lonc)

    for p in range(n_p):
        hs = [halo_rx[side, pl.ds(p * 2 * ch, 2 * ch), :].astype(F32) for side in range(2)]
        ns = [halo_rx[side, pl.ds(n_base + (p // 2) * 2 * ch, 2 * ch), :].astype(F32)[(p % 2) * ch : (p % 2 + 1) * ch]
              for side in range(2)]
        force0 = jnp.concatenate([noise[0, p].astype(F32), ns[0], ns[1]], axis=0)
        new = two_steps(fine[p].astype(F32), hs[0], hs[1], force0, noise[1, p].astype(F32), w1, w2, keep_f, lon)
        fin[p] = new
        diff = new.astype(F32) - obs_f[...].astype(F32)
        rows = jnp.sum(diff * diff, axis=1, keepdims=True)
        like = like + jnp.where(lane == p, scale_f * jnp.sum(rows * pf, axis=0, keepdims=True), 0.0)

    send1 = []
    for k in range(1, members):
        peer = lax.rem(me + k, members)
        send1.append(copy_to(tile(fin, lax.rem(peer, shares)), recv1.at[pl.ds(me * n_p, n_p)],
                             s1.at[k], r1.at[k], {"ens": peer}))
        send1[-1].start()
    own1 = pltpu.make_async_copy(tile(fin, rank), recv1.at[pl.ds(me * n_p, n_p)], loc.at[0])
    own1.start()

    pair_wait(edge, "recv")
    hs = [halo_rx[side, pl.ds(c_base, 2 * ch), :].astype(F32) for side in range(2)]
    force0 = jnp.concatenate([forcing_rows(0, 0, rc), edge_rx[0], edge_rx[1]], axis=0)
    new = two_steps(c0.astype(F32), hs[0], hs[1], force0, forcing_rows(1, 0, rc), w1c, w2c, keep_c, lonc)
    parts = []
    for p in range(n_p):
        mine = new[:, p * lonc : (p + 1) * lonc]
        parts.append(mine)
        diff = mine.astype(F32) - obs_c[...].astype(F32)
        rows = jnp.sum(diff * diff, axis=1, keepdims=True)
        like = like + jnp.where(lane == n_p + p, scale_c * jnp.sum(rows * pc, axis=0, keepdims=True), 0.0)
    likeb[band] = jnp.broadcast_to(like, likeb.shape[1:])
    send_b = []
    for k in range(1, bands):
        peer = lax.rem(band + k, bands)
        send_b.append(copy_to(likeb.at[band], likeb.at[band], bs.at[k], br.at[k], {"band": peer}))
        send_b[-1].start()

    n = n_p * rc
    lp = int(math.log2(piece))
    q = iota((n, n), 0)
    src = ((q >> lp) & (n_p - 1)) * rc + (q >> int(math.log2(n_p * piece))) * piece + (q & (piece - 1))
    cstage[...] = mm(onehot(iota((n, n), 1) == src), jnp.concatenate(parts, axis=0)).astype(BF16).reshape(cstage.shape)
    send_c = []
    for g in range(members // shares):
        for c in range(holders):
            peer = g * shares + holder(c)
            send_c.append((peer, copy_to(cstage.at[c], recvc.at[pl.ds(me * TILE_R, TILE_R)],
                                         cs1.at[g * holders + c], cr1.at[lax.rem(peer - me + members, members)],
                                         {"ens": peer})))
    for peer, desc in send_c:
        @pl.when(me != peer)
        def _():
            desc.start()

    for c in range(holders):
        @pl.when(rank == holder(c))
        def _():
            own = pltpu.make_async_copy(cstage.at[c], recvc.at[pl.ds(me * TILE_R, TILE_R)], loc.at[1])
            own.start()
            own.wait()

    own1.wait()
    for k in range(1, members):
        copy_to(tile(fin, rank), recv1.at[pl.ds(lax.rem(me - k + members, members) * n_p, n_p)],
                s1.at[k], r1.at[k], {"ens": lax.rem(me + k, members)}).wait_recv()
    send2 = []
    for k in list(range(1, shares)) + [0]:
        target = lax.rem(rank + k, shares)
        for s in range(n_p):
            slot = target * n_p + s
            chosen[slot] = recv1[par_s[0, group * n_p + slot]]
        from_ref = chosen.at[pl.ds(target * n_p, n_p)]
        if k:
            send2.append(copy_to(from_ref, tile(out_f, rank), s2.at[k], r2.at[k], {"ens": group + target}))
            send2[-1].start()
        else:
            own2 = pltpu.make_async_copy(from_ref, tile(out_f, rank), loc.at[0])
            own2.start()

    for k in range(1, bands):
        src_band = lax.rem(band - k + bands, bands)
        copy_to(likeb.at[src_band], likeb.at[src_band], bs.at[k], br.at[k],
                {"band": lax.rem(band + k, bands)}).wait_recv()
    whole = likeb[0]
    for b in range(1, bands):
        whole = whole + likeb[b]
    whole = whole[:1]
    likee[me] = whole
    send_l = []
    for k in range(1, members):
        send_l.append(copy_to(likee.at[me], likee.at[me], ls.at[k], lr.at[k], {"ens": lax.rem(me + k, members)}))
        send_l[-1].start()

    is_holder = functools.reduce(jnp.logical_or, [rank == holder(c) for c in range(holders)])
    n_slots = shares * n_p

    @pl.when(is_holder)
    def _():
        for k in range(1, members):
            copy_to(cstage.at[0], recvc.at[pl.ds(lax.rem(me - k + members, members) * TILE_R, TILE_R)],
                    cs1.at[0], cr1.at[k], {"ens": lax.rem(me + k, members)}).wait_recv()
        want = group * n_p + (iota((n_slots * piece, total), 0) >> lp)
        who = jnp.sum(jnp.where(dest[...] == want, parent, 0), axis=1, keepdims=True)
        inner = iota((n_slots * piece, 1), 0) & (piece - 1)
        pick = onehot(iota((n_slots * piece, total * piece), 1) == who * piece + inner)
        cchosen[...] = mm(pick, recvc[...]).astype(BF16).reshape(cchosen.shape)

    for c in range(holders):
        @pl.when(rank == holder(c))
        def _():
            for k in range(1, shares):
                target = lax.rem(rank + k, shares)
                copy_to(cchosen.at[target], recvc2.at[pl.ds(c * TILE_R, TILE_R)], cs2.at[k], cr2.at[c],
                        {"ens": group + target}).start()
            own = pltpu.make_async_copy(cchosen.at[rank], recvc2.at[pl.ds(c * TILE_R, TILE_R)], loc.at[1])
            own.start()
            own.wait()

    for k in range(1, members):
        src_m = lax.rem(me - k + members, members)
        copy_to(likee.at[src_m], likee.at[src_m], ls.at[k], lr.at[k], {"ens": lax.rem(me + k, members)}).wait_recv()
    everyone = likee[...].reshape(members, TILE_L)
    lane_all = iota((members, TILE_L), 1)
    for first, out in ((0, out_lf), (n_p, out_lc)):
        here = jnp.logical_and(lane_all >= first, lane_all < first + n_p)
        vals = jnp.where(here, everyone, -jnp.inf)
        peak = jnp.max(jnp.max(vals, axis=1, keepdims=True), axis=0, keepdims=True)
        part = jnp.where(here, jnp.exp(vals - peak), 0.0)
        norm = jnp.sum(jnp.sum(part, axis=1, keepdims=True), axis=0, keepdims=True)
        out[...] = (whole - (peak + jnp.log(norm)))[:, first : first + n_p]

    for c in range(holders):
        @pl.when(rank != holder(c))
        def _():
            copy_to(cchosen.at[0], recvc2.at[pl.ds(c * TILE_R, TILE_R)], cs2.at[0], cr2.at[c],
                    {"ens": group + holder(c)}).wait_recv()
    q = iota((n, n), 0)
    row = q & (rc - 1)
    src = (row >> lp) * (n_p * piece) + (q >> int(math.log2(rc))) * piece + (row & (piece - 1))
    out_c[...] = mm(onehot(iota((n, n), 1) == src), recvc2[...]).astype(BF16)

    own2.wait()
    for k in range(1, shares):
        source = lax.rem(rank - k + shares, shares)
        copy_to(chosen.at[pl.ds(0, n_p)], tile(out_f, source), s2.at[k], r2.at[k],
                {"ens": group + lax.rem(rank + k, shares)}).wait_recv()

    pair_wait(halo, "send")
    pair_wait(edge, "send")
    for desc in send1 + send2 + send_b + send_l:
        desc.wait_send()
    for peer, desc in send_c:
        @pl.when(me != peer)
        def _():
            desc.wait_send()

    @pl.when(is_holder)
    def _():
        for k in range(1, shares):
            copy_to(cchosen.at[0], recvc2.at[pl.ds(0, TILE_R)], cs2.at[k], cr2.at[0],
                    {"ens": group + lax.rem(rank + k, shares)}).wait_send()


def shards(fine, coarse, noise, kf, kc, obs_f, obs_c, prec_f, prec_c, offspring, dest_slot):
    bands, members = lax.axis_size("band"), lax.axis_size("ens")
    n_p, ch, hf, lon = fine.shape
    hc, lonc = coarse.shape[2:]
    rf, rc = ch * hf, ch * hc
    total = offspring.shape[0]
    shares = (rf // TILE_R) * (lon // TILE_L)
    holders = n_p * rc // TILE_R
    groups = members // shares
    lane_w = -(-total // TILE_L) * TILE_L
    halo_rows = n_p * 3 * ch + 2 * ch
    dma = pltpu.SemaphoreType.DMA
    vmem = pl.BlockSpec(memory_space=pltpu.VMEM)
    of, oc, lf, lc = pl.pallas_call(
        functools.partial(kernel, bands, members),
        out_shape=(
            jax.ShapeDtypeStruct((n_p, rf, lon), BF16),
            jax.ShapeDtypeStruct((n_p * rc, lonc), BF16),
            jax.ShapeDtypeStruct((1, n_p), F32),
            jax.ShapeDtypeStruct((1, n_p), F32),
        ),
        in_specs=[vmem] * 11,
        out_specs=(vmem,) * 4,
        scratch_shapes=[
            pltpu.VMEM((2, halo_rows, lon), BF16),
            pltpu.VMEM((2, halo_rows, lon), BF16),
            pltpu.VMEM((2, ch, n_p * lonc), F32),
            pltpu.VMEM((2, ch, n_p * lonc), F32),
            pltpu.VMEM((n_p, rf, lon), BF16),
            pltpu.VMEM((total, TILE_R, TILE_L), BF16),
            pltpu.VMEM((shares * n_p, TILE_R, TILE_L), BF16),
            pltpu.VMEM((holders, TILE_R, TILE_L), BF16),
            pltpu.VMEM((members * TILE_R, TILE_L), BF16),
            pltpu.VMEM((shares, TILE_R, TILE_L), BF16),
            pltpu.VMEM((holders * TILE_R, TILE_L), BF16),
            pltpu.VMEM((bands, 8, TILE_L), F32),
            pltpu.VMEM((members, 1, TILE_L), F32),
            pltpu.VMEM((1, lane_w), I32),
            pltpu.SMEM((1, lane_w), I32),
            dma((2,)), dma((2,)), dma((2,)), dma((2,)),
            dma((members,)), dma((members,)), dma((shares,)), dma((shares,)),
            dma((groups * holders,)), dma((members,)), dma((shares,)), dma((holders,)),
            dma((bands,)), dma((bands,)), dma((members,)), dma((members,)), dma((2,)),
        ],
        compiler_params=pltpu.CompilerParams(
            collective_id=0, has_side_effects=True, vmem_limit_bytes=40 * 1024 * 1024
        ),
    )(
        fine.reshape(n_p, rf, lon),
        coarse.reshape(n_p * rc, lonc),
        noise.reshape(2, n_p, rf, lon),
        kf, kc,
        obs_f.reshape(rf, lon),
        obs_c.reshape(rc, lonc),
        prec_f.reshape(1, hf),
        prec_c.reshape(1, hc),
        offspring.reshape(1, total),
        dest_slot.reshape(1, total),
    )
    return (
        of.reshape(n_p, ch, hf, lon),
        oc.reshape(n_p, ch, hc, lonc),
        lf.reshape(n_p),
        lc.reshape(n_p),
    )


def solution(mesh):
    return jax.shard_map(
        shards,
        mesh=mesh,
        in_specs=(
            P("ens", None, "band", None),
            P("ens", None, "band", None),
            P(None, "ens", None, "band", None),
            P(),
            P(),
            P(None, "band", None),
            P(None, "band", None),
            P("band"),
            P("band"),
            P(),
            P(),
        ),
        out_specs=(P("ens", None, "band", None), P("ens", None, "band", None), P("ens"), P("ens")),
        check_vma=False,
    )
```

time: 181 us -> 40 us (0.22)
  blocking collectives: 92.4 us -> 0 us
  starting transfers between devices: 33.3 us -> 0 us
  Pallas kernels: 0 us -> 29.7 us
  other arithmetic: 25.3 us -> 0 us
  local copies, waits for them, and re-layouts: 20.7 us -> 9.22 us
  between operations: 3.85 us -> 0.68 us
  matrix products: 2.62 us -> 0 us
    psum x2 -> x0, blocking collectives: 39.6 us -> none  [the longest x1 34.4 us: shards(): lax.psum((jnp.sum(jnp.exp(like_fine - peak_fine)), jnp.sum(jnp.exp(like_c...]
    pmax x1 -> x0, blocking collectives: 30.2 us -> none  [shards(): lax.pmax((jnp.max(like_fine), jnp.max(like_coarse)), 'ens')]
    pallas_call x0 -> x1, Pallas kernels: none -> 29.7 us  [shards(): pl.pallas_call(functools.partial(kernel, bands, members), out_shape=(jax....]
    ppermute x8 -> x0, starting transfers between devices: 23.8 us -> none  [the longest x4 18.7 us: padded_2(): lax.ppermute(lax.slice_in_dim(block, block.shape[dim] - width, None, axis...]
    all_gather x1 -> x0, blocking collectives: 22.5 us -> none  [shards(): everyone = lax.all_gather(coarse_state, 'ens', axis=0, tiled=True)]
    reduce_sum x6 -> x0, other arithmetic: 15.9 us -> none  [the longest x2 12.5 us: restrict(): return 4.0 * jnp.mean(blocks, axis=(3, 5))]
    convert_element_type x6 -> x0, local copies, waits for them, and re-layouts: 9.81 us -> none  [the longest x2 9.18 us: shards(): forcing = noise[step].astype(jnp.float32)]
    all_to_all x2 -> x0, starting transfers between devices: 9.47 us -> none  [the longest x1 5.94 us: shards(): lax.all_to_all(fine_flat, 'ens', split_axis=1, concat_axis=0, tiled=True)]
  transfers between devices with their start and end apart: 10 -> 0, of which waited for: 1 -> 0; matrix products, arithmetic and copies ran while one was open for 20% -> 0% of each run, Pallas kernels for 0% -> 0%
where the time goes in v1:
time: 40 us; the launch traced here: 39.6 us
  Pallas kernels  29.7 us (74%)
  local copies, waits for them, and re-layouts  9.22 us (23%)
  between operations  0.68 us (2%)
    pallas_call x1, Pallas kernels, shards(): pl.pallas_call(functools.partial(kernel, bands, members), out_shape=(jax....  29.7 us
    unnamed x26, local copies, waits for them, and re-layouts  9.22 us

profile of v1, /device:TPU:0, one launch (start us, length us, event | category | flops | bytes accessed | tf_op | source)
XLA Modules:
  0.0 39.6 jit_solution(12670328163101919215)
XLA Ops:
  0.6 0.0 copy-start.3
  0.6 0.0 copy-start.7
  0.7 0.0 copy-start.8
  0.7 0.7 %copy-done.3 = bf16[4,8,2,128]{3,2,1,0:T(2,128)(2,1)S(1)} copy-done((bf16[4,8,2,128]{3,2,1,0:T(2,128)(2,1)S(1)}, bf16[4,8,2,128]{3,2,1,0:T(2,128)(2,1)}, u32[]{:S(2)}) %copy-start.3) | copy-done | bytes 16408
  1.4 0.0 copy-done.7
  1.4 0.0 copy-done.8
  1.4 0.0 copy-start
  1.4 1.0 %copy-done = bf16[2,4,8,8,512]{4,3,2,1,0:T(8,128)(2,1)S(1)} copy-done((bf16[2,4,8,8,512]{4,3,2,1,0:T(8,128)(2,1)S(1)}, bf16[2,4,8,8,512]{4,3,2,1,0:T(8,128)(2,1)}, u32[]{:S(2)}) %copy-start) | copy-done | bytes 524312
  2.4 0.0 copy-start.1
  2.4 0.9 %copy-done.1 = bf16[4,8,8,512]{3,2,1,0:T(8,128)(2,1)S(1)} copy-done((bf16[4,8,8,512]{3,2,1,0:T(8,128)(2,1)S(1)}, bf16[4,8,8,512]{3,2,1,0:T(8,128)(2,1)}, u32[]{:S(2)}) %copy-start.1) | copy-done | bytes 262168
  3.4 0.0 copy-start.2
  3.4 0.8 %copy-done.2 = bf16[8,8,512]{2,1,0:T(8,128)(2,1)S(1)} copy-done((bf16[8,8,512]{2,1,0:T(8,128)(2,1)S(1)}, bf16[8,8,512]{2,1,0:T(8,128)(2,1)}, u32[]{:S(2)}) %copy-start.2) | copy-done | bytes 65560
  4.2 0.0 copy-start.4
  4.2 0.7 %copy-done.4 = bf16[8,2,128]{2,1,0:T(2,128)(2,1)S(1)} copy-done((bf16[8,2,128]{2,1,0:T(2,128)(2,1)S(1)}, bf16[8,2,128]{2,1,0:T(2,128)(2,1)}, u32[]{:S(2)}) %copy-start.4) | copy-done | bytes 4120
  4.9 0.0 copy-start.5
  4.9 0.7 %copy-done.5 = bf16[8,72]{1,0:T(8,128)(2,1)S(1)} copy-done((bf16[8,72]{1,0:T(8,128)(2,1)S(1)}, bf16[8,72]{1,0:T(8,128)(2,1)}, u32[]{:S(2)}) %copy-start.5) | copy-done | bytes 1176
  5.6 0.0 copy-start.6
  5.6 0.7 %copy-done.6 = bf16[8,72]{1,0:T(8,128)(2,1)S(1)} copy-done((bf16[8,72]{1,0:T(8,128)(2,1)S(1)}, bf16[8,72]{1,0:T(8,128)(2,1)}, u32[]{:S(2)}) %copy-start.6) | copy-done | bytes 1176
  6.2 0.0 copy-start.9
  6.2 0.7 %copy-done.9 = s32[64]{0:T(128)S(1)} copy-done((s32[64]{0:T(128)S(1)}, s32[64]{0:T(128)}, u32[]{:S(2)}) %copy-start.9) | copy-done | bytes 280
  6.9 0.0 copy-start.10
  6.9 0.7 %copy-done.10 = s32[64]{0:T(128)S(1)} copy-done((s32[64]{0:T(128)S(1)}, s32[64]{0:T(128)}, u32[]{:S(2)}) %copy-start.10) | copy-done | bytes 280
  7.6 29.7 %shard_map.138 = (bf16[4,64,512]{2,1,0:T(8,128)(2,1)S(1)}, bf16[64,128]{1,0:T(8,128)(2,1)S(1)}, f32[1,4]{1,0:T(1,128)S(1)}, f32[1,4]{1,0:T(1,128)S(1)}) custom-call(bf16[4,64,512]{2,1,0:T(8,128)(2,1)S(1)} %bitcast.14, bf16[64,128]{1,0:T(8,128)(2,1)S(1)} %bitcast.17, bf16[2,4,64,512]{3,2,1,0:T(8,128)(2,1)S(1)} %bitcast.13, bf16[8,72]{1,0:T(8,128)(2,1)S(1)} %copy-done.5, ...), custom_call_target="tpu_custom_call" | custom-call | tf_op jit(solution)/shard_map/pallas_call | solution.py:436
  37.3 0.7 %copy.19 = bf16[4,8,8,512]{3,2,1,0:T(8,128)(2,1)} copy(bf16[4,8,8,512]{3,2,1,0:T(8,128)(2,1)S(1)} %bitcast.15) | data formatting | bytes 524288
  38.0 0.6 %copy.20 = bf16[4,8,2,128]{3,2,1,0:T(2,128)(2,1)} copy(bf16[4,8,2,128]{3,2,1,0:T(2,128)(2,1)S(1)} %bitcast.18) | data formatting | bytes 32768
  38.6 0.5 %copy.21 = f32[4]{0:T(128)} copy(f32[4]{0:T(128)S(1)} %bitcast.25) | data formatting | bytes 32
  39.1 0.5 %copy.22 = f32[4]{0:T(128)} copy(f32[4]{0:T(128)S(1)} %bitcast.24) | data formatting | bytes 32
Async XLA Ops:
  0.6 0.7 %copy-start.3 = (bf16[4,8,2,128]{3,2,1,0:T(2,128)(2,1)S(1)}, bf16[4,8,2,128]{3,2,1,0:T(2,128)(2,1)}, u32[]{:S(2)}) copy-start(bf16[4,8,2,128]{3,2,1,0:T(2,128)(2,1)} %param.12) | copy-start | bytes 49156
  0.6 0.7 %copy-start.7 = (f32[8]{0:T(128)S(1)}, f32[8]{0:T(128)}, u32[]{:S(2)}) copy-start(f32[8]{0:T(128)} %param.18) | copy-start | bytes 100
  0.7 0.7 %copy-start.8 = (f32[2]{0:T(128)S(1)}, f32[2]{0:T(128)}, u32[]{:S(2)}) copy-start(f32[2]{0:T(128)} %param.19) | copy-start | bytes 28
  1.4 1.0 %copy-start = (bf16[2,4,8,8,512]{4,3,2,1,0:T(8,128)(2,1)S(1)}, bf16[2,4,8,8,512]{4,3,2,1,0:T(8,128)(2,1)}, u32[]{:S(2)}) copy-start(bf16[2,4,8,8,512]{4,3,2,1,0:T(8,128)(2,1)} %param.13) | copy-start | bytes 1572868
  2.4 0.9 %copy-start.1 = (bf16[4,8,8,512]{3,2,1,0:T(8,128)(2,1)S(1)}, bf16[4,8,8,512]{3,2,1,0:T(8,128)(2,1)}, u32[]{:S(2)}) copy-start(bf16[4,8,8,512]{3,2,1,0:T(8,128)(2,1)} %param.11) | copy-start | bytes 786436
  3.4 0.8 %copy-start.2 = (bf16[8,8,512]{2,1,0:T(8,128)(2,1)S(1)}, bf16[8,8,512]{2,1,0:T(8,128)(2,1)}, u32[]{:S(2)}) copy-start(bf16[8,8,512]{2,1,0:T(8,128)(2,1)} %param.16) | copy-start | bytes 196612
  4.2 0.7 %copy-start.4 = (bf16[8,2,128]{2,1,0:T(2,128)(2,1)S(1)}, bf16[8,2,128]{2,1,0:T(2,128)(2,1)}, u32[]{:S(2)}) copy-start(bf16[8,2,128]{2,1,0:T(2,128)(2,1)} %param.17) | copy-start | bytes 12292
  4.9 0.7 %copy-start.5 = (bf16[8,72]{1,0:T(8,128)(2,1)S(1)}, bf16[8,72]{1,0:T(8,128)(2,1)}, u32[]{:S(2)}) copy-start(bf16[8,72]{1,0:T(8,128)(2,1)} %kf.1) | copy-start | bytes 3460
  5.6 0.7 %copy-start.6 = (bf16[8,72]{1,0:T(8,128)(2,1)S(1)}, bf16[8,72]{1,0:T(8,128)(2,1)}, u32[]{:S(2)}) copy-start(bf16[8,72]{1,0:T(8,128)(2,1)} %kc.1) | copy-start | bytes 3460
  6.2 0.7 %copy-start.9 = (s32[64]{0:T(128)S(1)}, s32[64]{0:T(128)}, u32[]{:S(2)}) copy-start(s32[64]{0:T(128)} %param.20) | copy-start | bytes 772
  6.9 0.7 %copy-start.10 = (s32[64]{0:T(128)S(1)}, s32[64]{0:T(128)}, u32[]{:S(2)}) copy-start(s32[64]{0:T(128)} %param.21) | copy-start | bytes 772

commit v2 on v1

--- a/solution.py
+++ b/solution.py
@@ -13,6 +13,7 @@
 I32 = jnp.int32
 TILE_R = 16
 TILE_L = 128
+VMEM_LIMIT = 56 * 1024 * 1024
 
 
 def iota(shape, dim):
@@ -68,8 +69,9 @@
 
 def kernel(
     bands, members,
-    fine, coarse, noise, kf, kc, obs_f, obs_c, prec_f, prec_c, offs, dest,
+    fine_h, coarse_h, noise_h, kf_h, kc_h, obs_f_h, obs_c_h, prec_f_h, prec_c_h, offs_h, dest_h,
     out_f, out_c, out_lf, out_lc,
+    fine, coarse, noise, kf, kc, obs_f, obs_c, prec_f, prec_c, offs, dest, in_sem,
     halo_tx, halo_rx, edge_tx, edge_rx, fin, recv1, chosen, cstage, recvc, cchosen, recvc2,
     likeb, likee, par_v, par_s,
     h_send, h_recv, e_send, e_recv, s1, r1, s2, r2, cs1, cr1, cs2, cr2, bs, br, ls, lr, loc,
@@ -101,6 +103,12 @@
             device_id=device, device_id_type=pl.DeviceIdType.MESH,
         )
 
+    sources = (fine_h, noise_h, coarse_h, kf_h, kc_h, obs_f_h, obs_c_h, prec_f_h, prec_c_h, offs_h, dest_h)
+    places = (fine, noise, coarse, kf, kc, obs_f, obs_c, prec_f, prec_c, offs, dest)
+    loads = [pltpu.make_async_copy(a, b, in_sem.at[i]) for i, (a, b) in enumerate(zip(sources, places))]
+    for load in loads:
+        load.start()
+
     barrier = pltpu.get_barrier_semaphore()
     for k in range(1, members):
         pl.semaphore_signal(barrier, inc=1, device_id={"ens": lax.rem(me + k, members)},
@@ -121,6 +129,8 @@
     n_base = n_p * 2 * ch
     c_base = n_base + n_p * ch
     picked_noise = []
+    for load in loads[:3]:
+        load.wait()
     for p in range(n_p):
         rows = mm(sel_state, fine[p]).astype(BF16)
         halo_tx[0, pl.ds(p * 2 * ch, 2 * ch), :] = rows[: 2 * ch]
@@ -191,6 +201,8 @@
     def _():
         edge[1].start()
 
+    for load in loads[3:]:
+        load.wait()
     lane_w = par_v.shape[1]
     lanes = iota((total, total), 1)
     subs = iota((total, total), 0)
@@ -255,6 +267,15 @@
     like = jnp.zeros((1, TILE_L), F32)
     scale_f = -0.5 / math.sqrt(ch * hf * bands * lon)
     scale_c = -0.5 / math.sqrt(ch * hc * bands * lonc)
+
+    send1, own1 = [], []
+    batch = n_p // 2
+    part1 = lambda ref, first, b: ref.at[pl.ds(first * n_p + b * batch, batch)]
+
+    def share1(share, b):
+        row = pl.multiple_of((share // lane_blocks) * TILE_R, TILE_R)
+        at = pl.multiple_of((share % lane_blocks) * TILE_L, TILE_L)
+        return fin.at[pl.ds(b * batch, batch), pl.ds(row, TILE_R), pl.ds(at, TILE_L)]
 
     for p in range(n_p):
         hs = [halo_rx[side, pl.ds(p * 2 * ch, 2 * ch), :].astype(F32) for side in range(2)]
@@ -267,14 +288,15 @@
         rows = jnp.sum(diff * diff, axis=1, keepdims=True)
         like = like + jnp.where(lane == p, scale_f * jnp.sum(rows * pf, axis=0, keepdims=True), 0.0)
 
-    send1 = []
-    for k in range(1, members):
-        peer = lax.rem(me + k, members)
-        send1.append(copy_to(tile(fin, lax.rem(peer, shares)), recv1.at[pl.ds(me * n_p, n_p)],
-                             s1.at[k], r1.at[k], {"ens": peer}))
-        send1[-1].start()
-    own1 = pltpu.make_async_copy(tile(fin, rank), recv1.at[pl.ds(me * n_p, n_p)], loc.at[0])
-    own1.start()
+        if (p + 1) % batch == 0:
+            b = p // batch
+            for k in range(1, members):
+                peer = lax.rem(me + k, members)
+                send1.append(copy_to(share1(lax.rem(peer, shares), b), part1(recv1, me, b),
+                                     s1.at[b * members + k], r1.at[b * members + k], {"ens": peer}))
+                send1[-1].start()
+            own1.append(pltpu.make_async_copy(share1(rank, b), part1(recv1, me, b), loc.at[2 + b]))
+            own1[-1].start()
 
     pair_wait(edge, "recv")
     hs = [halo_rx[side, pl.ds(c_base, 2 * ch), :].astype(F32) for side in range(2)]
@@ -318,10 +340,12 @@
             own.start()
             own.wait()
 
-    own1.wait()
-    for k in range(1, members):
-        copy_to(tile(fin, rank), recv1.at[pl.ds(lax.rem(me - k + members, members) * n_p, n_p)],
-                s1.at[k], r1.at[k], {"ens": lax.rem(me + k, members)}).wait_recv()
+    for b in range(2):
+        own1[b].wait()
+        for k in range(1, members):
+            copy_to(share1(rank, b), part1(recv1, lax.rem(me - k + members, members), b),
+                    s1.at[b * members + k], r1.at[b * members + k],
+                    {"ens": lax.rem(me + k, members)}).wait_recv()
     send2 = []
     for k in list(range(1, shares)) + [0]:
         target = lax.rem(rank + k, shares)
@@ -420,6 +444,15 @@
                     {"ens": group + lax.rem(rank + k, shares)}).wait_send()
 
 
+def write_out(*refs):
+    count = (len(refs) - 1) // 2
+    copies = [pltpu.make_async_copy(refs[i], refs[count + i], refs[-1].at[i]) for i in range(count)]
+    for copy in copies:
+        copy.start()
+    for copy in copies:
+        copy.wait()
+
+
 def shards(fine, coarse, noise, kf, kc, obs_f, obs_c, prec_f, prec_c, offspring, dest_slot):
     bands, members = lax.axis_size("band"), lax.axis_size("ens")
     n_p, ch, hf, lon = fine.shape
@@ -433,17 +466,32 @@
     halo_rows = n_p * 3 * ch + 2 * ch
     dma = pltpu.SemaphoreType.DMA
     vmem = pl.BlockSpec(memory_space=pltpu.VMEM)
-    of, oc, lf, lc = pl.pallas_call(
+    hbm = pl.BlockSpec(memory_space=pl.ANY)
+    args = (
+        fine.reshape(n_p, rf, lon),
+        coarse.reshape(n_p * rc, lonc),
+        noise.reshape(2, n_p, rf, lon),
+        kf, kc,
+        obs_f.reshape(rf, lon),
+        obs_c.reshape(rc, lonc),
+        prec_f.reshape(1, hf),
+        prec_c.reshape(1, hc),
+        offspring.reshape(1, total),
+        dest_slot.reshape(1, total),
+    )
+    results = (
+        jax.ShapeDtypeStruct((n_p, rf, lon), BF16),
+        jax.ShapeDtypeStruct((n_p * rc, lonc), BF16),
+        jax.ShapeDtypeStruct((1, n_p), F32),
+        jax.ShapeDtypeStruct((1, n_p), F32),
+    )
+    done = pl.pallas_call(
         functools.partial(kernel, bands, members),
-        out_shape=(
-            jax.ShapeDtypeStruct((n_p, rf, lon), BF16),
-            jax.ShapeDtypeStruct((n_p * rc, lonc), BF16),
-            jax.ShapeDtypeStruct((1, n_p), F32),
-            jax.ShapeDtypeStruct((1, n_p), F32),
-        ),
-        in_specs=[vmem] * 11,
+        out_shape=results,
+        in_specs=[hbm] * 11,
         out_specs=(vmem,) * 4,
-        scratch_shapes=[
+        scratch_shapes=[pltpu.VMEM(a.shape, a.dtype) for a in args] + [
+            dma((11,)),
             pltpu.VMEM((2, halo_rows, lon), BF16),
             pltpu.VMEM((2, halo_rows, lon), BF16),
             pltpu.VMEM((2, ch, n_p * lonc), F32),
@@ -460,25 +508,21 @@
             pltpu.VMEM((1, lane_w), I32),
             pltpu.SMEM((1, lane_w), I32),
             dma((2,)), dma((2,)), dma((2,)), dma((2,)),
-            dma((members,)), dma((members,)), dma((shares,)), dma((shares,)),
+            dma((2 * members,)), dma((2 * members,)), dma((shares,)), dma((shares,)),
             dma((groups * holders,)), dma((members,)), dma((shares,)), dma((holders,)),
-            dma((bands,)), dma((bands,)), dma((members,)), dma((members,)), dma((2,)),
+            dma((bands,)), dma((bands,)), dma((members,)), dma((members,)), dma((4,)),
         ],
         compiler_params=pltpu.CompilerParams(
-            collective_id=0, has_side_effects=True, vmem_limit_bytes=40 * 1024 * 1024
+            collective_id=0, has_side_effects=True, vmem_limit_bytes=VMEM_LIMIT
         ),
-    )(
-        fine.reshape(n_p, rf, lon),
-        coarse.reshape(n_p * rc, lonc),
-        noise.reshape(2, n_p, rf, lon),
-        kf, kc,
-        obs_f.reshape(rf, lon),
-        obs_c.reshape(rc, lonc),
-        prec_f.reshape(1, hf),
-        prec_c.reshape(1, hc),
-        offspring.reshape(1, total),
-        dest_slot.reshape(1, total),
-    )
+    )(*args)
+    of, oc, lf, lc = pl.pallas_call(
+        write_out,
+        out_shape=results,
+        in_specs=[hbm] * 4,
+        out_specs=(hbm,) * 4,
+        scratch_shapes=[dma((4,))],
+    )(*done)
     return (
         of.reshape(n_p, ch, hf, lon),
         oc.reshape(n_p, ch, hc, lonc),

time: 40 us -> 41.7 us (1.042)
  Pallas kernels: 29.7 us -> 40.9 us
  local copies, waits for them, and re-layouts: 9.22 us -> 0 us
    pallas_call x1 -> x2, Pallas kernels: 29.7 us -> 40.9 us  [the longest x1 31.3 us: shards(): pl.pallas_call(functools.partial(kernel, bands, members), out_shape=resul...]
    unnamed x26 -> x0, local copies, waits for them, and re-layouts: 9.22 us -> none
where the time goes in v2:
time: 41.7 us; the launch traced here: 41.6 us
  Pallas kernels  40.9 us (98%)
  between operations  0.64 us (2%)
    pallas_call x1, Pallas kernels, shards(): pl.pallas_call(functools.partial(kernel, bands, members), out_shape=resul...  31.3 us
    pallas_call x1, Pallas kernels, shards(): pl.pallas_call(write_out, out_shape=results, in_specs=[hbm] * 4, out_spec...  9.61 us

profile of v2, /device:TPU:0, one launch (start us, length us, event | category | flops | bytes accessed | tf_op | source)
XLA Modules:
  0.0 41.6 jit_solution(2925076431178743475)
XLA Ops:
  0.6 31.3 %shard_map.138 = (bf16[4,64,512]{2,1,0:T(8,128)(2,1)}, bf16[64,128]{1,0:T(8,128)(2,1)}, f32[1,4]{1,0:T(1,128)}, f32[1,4]{1,0:T(1,128)}) custom-call(bf16[4,64,512]{2,1,0:T(8,128)(2,1)} %bitcast.14, bf16[64,128]{1,0:T(8,128)(2,1)} %bitcast.16, bf16[2,4,64,512]{3,2,1,0:T(8,128)(2,1)} %bitcast.13, bf16[8,72]{1,0:T(8,128)(2,1)} %kf_h.1, bf16[8,72]{1,0:T(8,128)(2,1)} %kc_h.1, ...), custom_call_target="tpu_custom_call" | custom-call | tf_op jit(solution)/shard_map/pallas_call | solution.py:488
  32.0 9.6 %shard_map.139 = (bf16[4,64,512]{2,1,0:T(8,128)(2,1)}, bf16[64,128]{1,0:T(8,128)(2,1)}, f32[1,4]{1,0:T(1,128)}, f32[1,4]{1,0:T(1,128)}) custom-call(bf16[4,64,512]{2,1,0:T(8,128)(2,1)} %get-tuple-element.12.refs_0_, bf16[64,128]{1,0:T(8,128)(2,1)} %get-tuple-element.13.refs_1_, f32[1,4]{1,0:T(1,128)} %get-tuple-element.14.refs_2_, ...), custom_call_target="tpu_custom_call" | custom-call | tf_op jit(solution)/shard_map/pallas_call | solution.py:519

commit v3 on v2

--- a/solution.py
+++ b/solution.py
@@ -487,7 +487,7 @@
     )
     done = pl.pallas_call(
         functools.partial(kernel, bands, members),
-        out_shape=results,
+        out_shape=tuple(pltpu.VMEM(r.shape, r.dtype) for r in results),
         in_specs=[hbm] * 11,
         out_specs=(vmem,) * 4,
         scratch_shapes=[pltpu.VMEM(a.shape, a.dtype) for a in args] + [
@@ -519,10 +519,11 @@
     of, oc, lf, lc = pl.pallas_call(
         write_out,
         out_shape=results,
-        in_specs=[hbm] * 4,
+        in_specs=[vmem] * 4,
         out_specs=(hbm,) * 4,
         scratch_shapes=[dma((4,))],
-    )(*done)
+        compiler_params=pltpu.CompilerParams(vmem_limit_bytes=4 * 1024 * 1024),
+    )(*[pltpu.with_memory_space_constraint(d, pltpu.VMEM) for d in done])
     return (
         of.reshape(n_p, ch, hf, lon),
         oc.reshape(n_p, ch, hc, lonc),

time: 41.7 us -> 32.2 us (0.77)
  Pallas kernels: 40.9 us -> 31.4 us
    pallas_call x2, Pallas kernels: 40.9 us -> 31.4 us  [the longest x1 30.6 us: shards(): pl.pallas_call(functools.partial(kernel, bands, members), out_shape=tuple...]
where the time goes in v3:
time: 32.2 us; the launch traced here: 32 us
  Pallas kernels  31.4 us (98%)
  between operations  0.64 us (2%)
    pallas_call x1, Pallas kernels, shards(): pl.pallas_call(functools.partial(kernel, bands, members), out_shape=tuple...  30.6 us
    pallas_call x1, Pallas kernels, shards(): pl.pallas_call(write_out, out_shape=results, in_specs=[vmem] * 4, out_spe...  0.75 us

profile of v3, /device:TPU:0, one launch (start us, length us, event | category | flops | bytes accessed | tf_op | source)
XLA Modules:
  0.0 32.0 jit_solution(9404461190083136385)
XLA Ops:
  0.6 30.6 %shard_map.138 = (bf16[4,64,512]{2,1,0:T(8,128)(2,1)S(1)}, bf16[64,128]{1,0:T(8,128)(2,1)S(1)}, f32[1,4]{1,0:T(1,128)S(1)}, f32[1,4]{1,0:T(1,128)S(1)}) custom-call(bf16[4,64,512]{2,1,0:T(8,128)(2,1)} %bitcast.14, bf16[64,128]{1,0:T(8,128)(2,1)} %bitcast.16, bf16[2,4,64,512]{3,2,1,0:T(8,128)(2,1)} %bitcast.13, bf16[8,72]{1,0:T(8,128)(2,1)} %kf_h.1, ...), custom_call_target="tpu_custom_call" | custom-call | tf_op jit(solution)/shard_map/pallas_call | solution.py:488
  31.3 0.7 %shard_map.139 = (bf16[4,64,512]{2,1,0:T(8,128)(2,1)}, bf16[64,128]{1,0:T(8,128)(2,1)}, f32[1,4]{1,0:T(1,128)}, f32[1,4]{1,0:T(1,128)}) custom-call(bf16[4,64,512]{2,1,0:T(8,128)(2,1)S(1)} %get-tuple-element.12.refs_0_, bf16[64,128]{1,0:T(8,128)(2,1)S(1)} %get-tuple-element.13.refs_1_, f32[1,4]{1,0:T(1,128)S(1)} %get-tuple-element.14.refs_2_, ...), custom_call_target="tpu_custom_call" | custom-call | tf_op jit(solution)/shard_map/pallas_call | solution.py:519

commit v4 on v3

--- a/solution.py
+++ b/solution.py
@@ -65,6 +65,10 @@
     right = [pltpu.roll(v, width - 1, 1) for v in parts]
     join = lambda vs: vs[0] if len(vs) == 1 else jnp.concatenate(vs, axis=1)
     return jnp.concatenate([join(left), x, join(right)], axis=0).astype(BF16)
+
+
+def far_first(count):
+    return sorted(range(1, count), key=lambda k: (abs(k - count // 2), k))
 
 
 def kernel(
@@ -290,7 +294,7 @@
 
         if (p + 1) % batch == 0:
             b = p // batch
-            for k in range(1, members):
+            for k in far_first(members):
                 peer = lax.rem(me + k, members)
                 send1.append(copy_to(share1(lax.rem(peer, shares), b), part1(recv1, me, b),
                                      s1.at[b * members + k], r1.at[b * members + k], {"ens": peer}))
@@ -340,26 +344,6 @@
             own.start()
             own.wait()
 
-    for b in range(2):
-        own1[b].wait()
-        for k in range(1, members):
-            copy_to(share1(rank, b), part1(recv1, lax.rem(me - k + members, members), b),
-                    s1.at[b * members + k], r1.at[b * members + k],
-                    {"ens": lax.rem(me + k, members)}).wait_recv()
-    send2 = []
-    for k in list(range(1, shares)) + [0]:
-        target = lax.rem(rank + k, shares)
-        for s in range(n_p):
-            slot = target * n_p + s
-            chosen[slot] = recv1[par_s[0, group * n_p + slot]]
-        from_ref = chosen.at[pl.ds(target * n_p, n_p)]
-        if k:
-            send2.append(copy_to(from_ref, tile(out_f, rank), s2.at[k], r2.at[k], {"ens": group + target}))
-            send2[-1].start()
-        else:
-            own2 = pltpu.make_async_copy(from_ref, tile(out_f, rank), loc.at[0])
-            own2.start()
-
     for k in range(1, bands):
         src_band = lax.rem(band - k + bands, bands)
         copy_to(likeb.at[src_band], likeb.at[src_band], bs.at[k], br.at[k],
@@ -374,18 +358,38 @@
         send_l.append(copy_to(likee.at[me], likee.at[me], ls.at[k], lr.at[k], {"ens": lax.rem(me + k, members)}))
         send_l[-1].start()
 
+    for b in range(2):
+        own1[b].wait()
+        for k in range(1, members):
+            copy_to(share1(rank, b), part1(recv1, lax.rem(me - k + members, members), b),
+                    s1.at[b * members + k], r1.at[b * members + k],
+                    {"ens": lax.rem(me + k, members)}).wait_recv()
+    send2 = []
+    for k in far_first(shares) + [0]:
+        target = lax.rem(rank + k, shares)
+        for s in range(n_p):
+            slot = target * n_p + s
+            chosen[slot] = recv1[par_s[0, group * n_p + slot]]
+        from_ref = chosen.at[pl.ds(target * n_p, n_p)]
+        if k:
+            send2.append(copy_to(from_ref, tile(out_f, rank), s2.at[k], r2.at[k], {"ens": group + target}))
+            send2[-1].start()
+        else:
+            own2 = pltpu.make_async_copy(from_ref, tile(out_f, rank), loc.at[0])
+            own2.start()
+
     is_holder = functools.reduce(jnp.logical_or, [rank == holder(c) for c in range(holders)])
     n_slots = shares * n_p
 
     @pl.when(is_holder)
     def _():
-        for k in range(1, members):
-            copy_to(cstage.at[0], recvc.at[pl.ds(lax.rem(me - k + members, members) * TILE_R, TILE_R)],
-                    cs1.at[0], cr1.at[k], {"ens": lax.rem(me + k, members)}).wait_recv()
         want = group * n_p + (iota((n_slots * piece, total), 0) >> lp)
         who = jnp.sum(jnp.where(dest[...] == want, parent, 0), axis=1, keepdims=True)
         inner = iota((n_slots * piece, 1), 0) & (piece - 1)
         pick = onehot(iota((n_slots * piece, total * piece), 1) == who * piece + inner)
+        for k in range(1, members):
+            copy_to(cstage.at[0], recvc.at[pl.ds(lax.rem(me - k + members, members) * TILE_R, TILE_R)],
+                    cs1.at[0], cr1.at[k], {"ens": lax.rem(me + k, members)}).wait_recv()
         cchosen[...] = mm(pick, recvc[...]).astype(BF16).reshape(cchosen.shape)
 
     for c in range(holders):

time: 32.2 us -> 31.1 us (0.966)
  Pallas kernels: 31.4 us -> 30.3 us
    pallas_call x1, Pallas kernels: 30.6 us -> 29.5 us  [shards(): pl.pallas_call(functools.partial(kernel, bands, members), out_shape=tuple...]
where the time goes in v4:
time: 31.1 us; the launch traced here: 30.9 us
  Pallas kernels  30.3 us (97%)
  between operations  0.64 us (2%)
    pallas_call x1, Pallas kernels, shards(): pl.pallas_call(functools.partial(kernel, bands, members), out_shape=tuple...  29.5 us
    pallas_call x1, Pallas kernels, shards(): pl.pallas_call(write_out, out_shape=results, in_specs=[vmem] * 4, out_spe...  0.75 us

profile of v4, /device:TPU:0, one launch (start us, length us, event | category | flops | bytes accessed | tf_op | source)
XLA Modules:
  0.0 30.9 jit_solution(8208075781400168891)
XLA Ops:
  0.6 29.5 %shard_map.138 = (bf16[4,64,512]{2,1,0:T(8,128)(2,1)S(1)}, bf16[64,128]{1,0:T(8,128)(2,1)S(1)}, f32[1,4]{1,0:T(1,128)S(1)}, f32[1,4]{1,0:T(1,128)S(1)}) custom-call(bf16[4,64,512]{2,1,0:T(8,128)(2,1)} %bitcast.14, bf16[64,128]{1,0:T(8,128)(2,1)} %bitcast.16, bf16[2,4,64,512]{3,2,1,0:T(8,128)(2,1)} %bitcast.13, bf16[8,72]{1,0:T(8,128)(2,1)} %kf_h.1, ...), custom_call_target="tpu_custom_call" | custom-call | tf_op jit(solution)/shard_map/pallas_call | solution.py:492
  30.1 0.7 %shard_map.139 = (bf16[4,64,512]{2,1,0:T(8,128)(2,1)}, bf16[64,128]{1,0:T(8,128)(2,1)}, f32[1,4]{1,0:T(1,128)}, f32[1,4]{1,0:T(1,128)}) custom-call(bf16[4,64,512]{2,1,0:T(8,128)(2,1)S(1)} %get-tuple-element.12.refs_0_, bf16[64,128]{1,0:T(8,128)(2,1)S(1)} %get-tuple-element.13.refs_1_, f32[1,4]{1,0:T(1,128)S(1)} %get-tuple-element.14.refs_2_, ...), custom_call_target="tpu_custom_call" | custom-call | tf_op jit(solution)/shard_map/pallas_call | solution.py:523

commit v5 on v4

--- a/solution.py
+++ b/solution.py
@@ -273,7 +273,7 @@
     scale_c = -0.5 / math.sqrt(ch * hc * bands * lonc)
 
     send1, own1 = [], []
-    batch = n_p // 2
+    batch = 1
     part1 = lambda ref, first, b: ref.at[pl.ds(first * n_p + b * batch, batch)]
 
     def share1(share, b):
@@ -358,7 +358,7 @@
         send_l.append(copy_to(likee.at[me], likee.at[me], ls.at[k], lr.at[k], {"ens": lax.rem(me + k, members)}))
         send_l[-1].start()
 
-    for b in range(2):
+    for b in range(n_p // batch):
         own1[b].wait()
         for k in range(1, members):
             copy_to(share1(rank, b), part1(recv1, lax.rem(me - k + members, members), b),
@@ -512,9 +512,9 @@
             pltpu.VMEM((1, lane_w), I32),
             pltpu.SMEM((1, lane_w), I32),
             dma((2,)), dma((2,)), dma((2,)), dma((2,)),
-            dma((2 * members,)), dma((2 * members,)), dma((shares,)), dma((shares,)),
+            dma((n_p * members,)), dma((n_p * members,)), dma((shares,)), dma((shares,)),
             dma((groups * holders,)), dma((members,)), dma((shares,)), dma((holders,)),
-            dma((bands,)), dma((bands,)), dma((members,)), dma((members,)), dma((4,)),
+            dma((bands,)), dma((bands,)), dma((members,)), dma((members,)), dma((2 + n_p,)),
         ],
         compiler_params=pltpu.CompilerParams(
             collective_id=0, has_side_effects=True, vmem_limit_bytes=VMEM_LIMIT

time: 31.1 us -> 31.6 us (1.016)
  Pallas kernels: 30.3 us -> 30.8 us
    pallas_call x1, Pallas kernels: 29.5 us -> 30.1 us  [shards(): pl.pallas_call(functools.partial(kernel, bands, members), out_shape=tuple...]
where the time goes in v5:
time: 31.6 us; the launch traced here: 31.4 us
  Pallas kernels  30.8 us (97%)
  between operations  0.64 us (2%)
    pallas_call x1, Pallas kernels, shards(): pl.pallas_call(functools.partial(kernel, bands, members), out_shape=tuple...  30.1 us
    pallas_call x1, Pallas kernels, shards(): pl.pallas_call(write_out, out_shape=results, in_specs=[vmem] * 4, out_spe...  0.75 us

profile of v5, /device:TPU:0, one launch (start us, length us, event | category | flops | bytes accessed | tf_op | source)
XLA Modules:
  0.0 31.4 jit_solution(18212772715434146693)
XLA Ops:
  0.6 30.1 %shard_map.138 = (bf16[4,64,512]{2,1,0:T(8,128)(2,1)S(1)}, bf16[64,128]{1,0:T(8,128)(2,1)S(1)}, f32[1,4]{1,0:T(1,128)S(1)}, f32[1,4]{1,0:T(1,128)S(1)}) custom-call(bf16[4,64,512]{2,1,0:T(8,128)(2,1)} %bitcast.14, bf16[64,128]{1,0:T(8,128)(2,1)} %bitcast.16, bf16[2,4,64,512]{3,2,1,0:T(8,128)(2,1)} %bitcast.13, bf16[8,72]{1,0:T(8,128)(2,1)} %kf_h.1, ...), custom_call_target="tpu_custom_call" | custom-call | tf_op jit(solution)/shard_map/pallas_call | solution.py:492
  30.7 0.7 %shard_map.139 = (bf16[4,64,512]{2,1,0:T(8,128)(2,1)}, bf16[64,128]{1,0:T(8,128)(2,1)}, f32[1,4]{1,0:T(1,128)}, f32[1,4]{1,0:T(1,128)}) custom-call(bf16[4,64,512]{2,1,0:T(8,128)(2,1)S(1)} %get-tuple-element.12.refs_0_, bf16[64,128]{1,0:T(8,128)(2,1)S(1)} %get-tuple-element.13.refs_1_, f32[1,4]{1,0:T(1,128)S(1)} %get-tuple-element.14.refs_2_, ...), custom_call_target="tpu_custom_call" | custom-call | tf_op jit(solution)/shard_map/pallas_call | solution.py:523
